TPU v7x, 32 devices: a whole 2x2x4 slice. The times are simulated.
32 devices in a mesh: groups: 2 (over y), rows: 4 (over z), chan: 2 (over x), sub: 2 (over core).
Axes of the slice: x: 2, y: 2, z: 4, core: 2. Of those that a mesh axis runs over, the one named last changes fastest.
Arguments:
- pair: bfloat16 [96, 48, 128], P(('groups', 'rows'), ('chan', 'sub')), parts along dimension 0, may hold values from -6 to 6
- res_mask: int32 [96], P('groups'), parts along dimension 0, may hold values 0 or 1
- out_ab: bfloat16 [128, 512], replicated, may hold values from -0.5 to 0.5
- out_gate: bfloat16 [128, 128], replicated, may hold values from -0.5 to 0.5
- out_proj: bfloat16 [128, 128], replicated, may hold values from -0.5 to 0.5
- in_ab: bfloat16 [128, 512], replicated, may hold values from -0.5 to 0.5
- in_gate: bfloat16 [128, 128], replicated, may hold values from -0.5 to 0.5
- in_proj: bfloat16 [128, 128], replicated, may hold values from -0.5 to 0.5
Outputs:
- updated: bfloat16 [96, 48, 128], P(('groups', 'rows'), ('chan', 'sub')), parts along dimension 0
There are 2 independent parts, one for each index of `groups`. A program takes and returns all parts, laid end to end along the dimension named above; an argument that names none is the same for every part. Nothing has to cross between parts.
All inputs are finite; a program needn't handle non-finite values.
Results may differ from a plain program's by a relative error of at most 0.012.
Values may be sent and summed in bfloat16 or wider, within the bound.
A program may use at most 64 MiB of HBM per device.

v0:
```python
import jax
import jax.numpy as jnp
from jax import lax
from jax.sharding import PartitionSpec as P


def normalize(values, axis):
    mean = jnp.mean(values, axis=axis, keepdims=True)
    centered = values - mean
    var = jnp.mean(centered * centered, axis=axis, keepdims=True)
    return centered * lax.rsqrt(var + 1e-05)


def prepare(pair_in, res_mask, w_ab, w_gate):
    row_count = pair_in.shape[0]
    col_count = pair_in.shape[1]
    hidden = w_ab.shape[1] // 4
    pair_f = pair_in.astype(jnp.float32)
    normed = normalize(pair_f, -1).astype(jnp.bfloat16)
    proj = jnp.einsum("ijc,cd->dij", normed, w_ab, preferred_element_type=jnp.float32)
    row_start = lax.axis_index("rows") * row_count
    col_start = lax.axis_index(("chan", "sub")) * col_count
    row_mask = lax.dynamic_slice_in_dim(res_mask, row_start, row_count).astype(jnp.float32)
    col_mask = lax.dynamic_slice_in_dim(res_mask, col_start, col_count).astype(jnp.float32)
    pair_mask = row_mask[:, None] * col_mask[None, :]
    left = (jax.nn.sigmoid(proj[:hidden]) * proj[hidden : 2 * hidden] * pair_mask).astype(
        jnp.bfloat16
    )
    right = (jax.nn.sigmoid(proj[2 * hidden : 3 * hidden]) * proj[3 * hidden :] * pair_mask).astype(
        jnp.bfloat16
    )
    gate = jax.nn.sigmoid(
        jnp.einsum("ijc,ce->ije", normed, w_gate, preferred_element_type=jnp.float32)
    )
    return (pair_f, left, right, gate)


def finish(pair_f, tri_local, gate, w_proj):
    tnorm = normalize(tri_local.astype(jnp.float32), 0).astype(jnp.bfloat16)
    update = jnp.einsum("dij,de->ije", tnorm, w_proj, preferred_element_type=jnp.float32)
    return (pair_f + gate * update).astype(jnp.bfloat16)


def on_device(pair, res_mask, out_ab, out_gate, out_proj, in_ab, in_gate, in_proj):
    pair_f, left, right, gate = prepare(pair, res_mask, out_ab, out_gate)
    left_grp, right_grp = (
        lax.all_to_all(left, ("chan", "sub"), split_axis=0, concat_axis=2, tiled=True),
        lax.all_to_all(right, ("chan", "sub"), split_axis=0, concat_axis=2, tiled=True),
    )
    tri = jnp.einsum(
        "dik,djk->dij",
        left_grp,
        lax.all_gather(right_grp, "rows", axis=1, tiled=True),
        preferred_element_type=jnp.float32,
    ).astype(jnp.bfloat16)
    tri_local = lax.all_to_all(tri, ("chan", "sub"), split_axis=2, concat_axis=0, tiled=True)
    middle = finish(pair_f, tri_local, gate, out_proj)
    mid_f, left, right, gate = prepare(middle, res_mask, in_ab, in_gate)
    left_grp, right_grp = (
        lax.all_to_all(left, ("chan", "sub"), split_axis=0, concat_axis=2, tiled=True),
        lax.all_to_all(right, ("chan", "sub"), split_axis=0, concat_axis=2, tiled=True),
    )
    left_turned = lax.all_to_all(left_grp, "rows", split_axis=2, concat_axis=1, tiled=True)
    tri = jnp.einsum(
        "dki,dkj->dij",
        left_turned,
        lax.all_gather(right_grp, "rows", axis=1, tiled=True),
        preferred_element_type=jnp.float32,
    ).astype(jnp.bfloat16)
    tri_local = lax.all_to_all(tri, ("chan", "sub"), split_axis=2, concat_axis=0, tiled=True)
    return finish(mid_f, tri_local, gate, in_proj)


def solution(mesh):
    return jax.shard_map(
        on_device,
        mesh=mesh,
        in_specs=(
            P(("groups", "rows"), ("chan", "sub"), None),
            P("groups"),
            P(),
            P(),
            P(),
            P(),
            P(),
            P(),
        ),
        out_specs=P(("groups", "rows"), ("chan", "sub"), None),
        check_vma=False,
    )
```

profile of v0, /device:TPU:0, one launch (start us, length us, event | category | flops | bytes accessed | tf_op | source)
XLA Modules:
  0.0 97.5 jit_solution(16503399892038843851)
XLA Ops:
  0.0 1.0 convert_reduce_fusion
  2.1 0.5 copy.84
  2.6 1.1 %reshape.100 = bf16[4,2,2304]{2,1,0:T(2,128)(2,1)} reshape(bf16[128,12,12]{2,1,0:T(8,128)(2,1)S(1)} %copy.84) | data formatting | bytes 73728
  3.7 4.2 %all-to-all-start = ((bf16[4,2,2304]{2,1,0:T(2,128)(2,1)}), bf16[4,2,2304]{2,1,0:T(2,128)(2,1)S(1)}, u32[]{:S(2)}, u32[]{:S(2)}) async-start(bf16[4,2,2304]{2,1,0:T(2,128)(2,1)} %reshape.100), calls=%async_computation | async-start | bytes 73728 | tf_op jit(solution)/shard_map/all_to_all | solution.py:47
  8.4 1.1 %reshape.102 = bf16[4,2,2304]{2,1,0:T(2,128)(2,1)} reshape(bf16[128,12,12]{2,1,0:T(8,128)(2,1)S(1)} %copy.86) | data formatting | bytes 73728
  9.5 2.4 %all-to-all-done = bf16[4,2,2304]{2,1,0:T(2,128)(2,1)S(1)} async-done(((bf16[4,2,2304]{2,1,0:T(2,128)(2,1)}), bf16[4,2,2304]{2,1,0:T(2,128)(2,1)S(1)}, u32[]{:S(2)}, u32[]{:S(2)}) %all-to-all-start) | async-done | bytes 36896 | tf_op jit(solution)/shard_map/all_to_all | solution.py:47
  11.9 3.3 %all-to-all-start.1 = ((bf16[4,2,2304]{2,1,0:T(2,128)(2,1)}), bf16[4,2,2304]{2,1,0:T(2,128)(2,1)S(1)}, u32[]{:S(2)}, u32[]{:S(2)}) async-start(bf16[4,2,2304]{2,1,0:T(2,128)(2,1)} %reshape.102), calls=%async_computation.1 | async-start | bytes 73728 | tf_op jit(solution)/shard_map/all_to_all | solution.py:48
  15.6 0.5 copy.85
  16.4 2.7 %all-to-all-done.1 = bf16[4,2,2304]{2,1,0:T(2,128)(2,1)S(1)} async-done(((bf16[4,2,2304]{2,1,0:T(2,128)(2,1)}), bf16[4,2,2304]{2,1,0:T(2,128)(2,1)S(1)}, u32[]{:S(2)}, u32[]{:S(2)}) %all-to-all-start.1) | async-done | bytes 36896 | tf_op jit(solution)/shard_map/all_to_all | solution.py:48
  19.5 0.5 copy.87
  20.3 15.4 %all_gather.6 = bf16[32,48,48]{2,0,1:T(8,128)(2,1)S(1)} all-gather(bf16[32,12,48]{2,0,1:T(8,128)(2,1)S(1)} %copy.88), channel_id=1, replica_groups=mesh['groups'=2,'rows'=4,'chan'=2,'sub'=2] {'rows'}, dimensions={1}, use_global_device_ids=true | all-gather | bytes 184320 | tf_op jit(solution)/shard_map/all_gather | solution.py:53
  36.3 0.8 reshape.104
  37.1 3.4 %all-to-all-start.2 = ((bf16[4,2,2304]{2,1,0:T(2,128)(2,1)}), bf16[4,2,2304]{2,1,0:T(2,128)(2,1)S(1)}, u32[]{:S(2)}, u32[]{:S(2)}) async-start(bf16[4,2,2304]{2,1,0:T(2,128)(2,1)} %reshape.104), calls=%async_computation.2 | async-start | bytes 73728 | tf_op jit(solution)/shard_map/all_to_all | solution.py:56
  40.7 3.7 %all-to-all-done.2 = bf16[4,2,2304]{2,1,0:T(2,128)(2,1)S(1)} async-done(((bf16[4,2,2304]{2,1,0:T(2,128)(2,1)}), bf16[4,2,2304]{2,1,0:T(2,128)(2,1)S(1)}, u32[]{:S(2)}, u32[]{:S(2)}) %all-to-all-start.2) | async-done | bytes 36896 | tf_op jit(solution)/shard_map/all_to_all | solution.py:56
  45.6 0.5 copy-done.3
  46.7 0.7 copy-done.2
  48.2 1.1 %reshape.106 = bf16[4,2,2304]{2,1,0:T(2,128)(2,1)} reshape(bf16[128,12,12]{2,1,0:T(8,128)(2,1)S(1)} %copy.95) | data formatting | bytes 73728
  49.3 3.3 %all-to-all-start.3 = ((bf16[4,2,2304]{2,1,0:T(2,128)(2,1)}), bf16[4,2,2304]{2,1,0:T(2,128)(2,1)S(1)}, u32[]{:S(2)}, u32[]{:S(2)}) async-start(bf16[4,2,2304]{2,1,0:T(2,128)(2,1)} %reshape.106), calls=%async_computation.3 | async-start | bytes 73728 | tf_op jit(solution)/shard_map/all_to_all | solution.py:60
  53.0 1.1 %reshape.110 = bf16[4,2,2304]{2,1,0:T(2,128)(2,1)} reshape(bf16[128,12,12]{2,1,0:T(8,128)(2,1)S(1)} %copy.100) | data formatting | bytes 73728
  54.1 2.4 %all-to-all-done.3 = bf16[4,2,2304]{2,1,0:T(2,128)(2,1)S(1)} async-done(((bf16[4,2,2304]{2,1,0:T(2,128)(2,1)}), bf16[4,2,2304]{2,1,0:T(2,128)(2,1)S(1)}, u32[]{:S(2)}, u32[]{:S(2)}) %all-to-all-start.3) | async-done | bytes 36896 | tf_op jit(solution)/shard_map/all_to_all | solution.py:60
  56.5 3.3 %all-to-all-start.5 = ((bf16[4,2,2304]{2,1,0:T(2,128)(2,1)}), bf16[4,2,2304]{2,1,0:T(2,128)(2,1)S(1)}, u32[]{:S(2)}, u32[]{:S(2)}) async-start(bf16[4,2,2304]{2,1,0:T(2,128)(2,1)} %reshape.110), calls=%async_computation.5 | async-start | bytes 73728 | tf_op jit(solution)/shard_map/all_to_all | solution.py:61
  60.2 0.6 copy.109
  60.8 0.8 reshape.108
  61.7 2.0 %all-to-all-done.5 = bf16[4,2,2304]{2,1,0:T(2,128)(2,1)S(1)} async-done(((bf16[4,2,2304]{2,1,0:T(2,128)(2,1)}), bf16[4,2,2304]{2,1,0:T(2,128)(2,1)S(1)}, u32[]{:S(2)}, u32[]{:S(2)}) %all-to-all-start.5) | async-done | bytes 36896 | tf_op jit(solution)/shard_map/all_to_all | solution.py:61
  63.7 5.4 %all-to-all-start.4 = ((bf16[4,2,2304]{2,1,0:T(2,128)(2,1)}), bf16[4,2,2304]{2,1,0:T(2,128)(2,1)S(1)}, u32[]{:S(2)}, u32[]{:S(2)}) async-start(bf16[4,2,2304]{2,1,0:T(2,128)(2,1)} %reshape.108), calls=%async_computation.4 | async-start | bytes 73728 | tf_op jit(solution)/shard_map/all_to_all | solution.py:63
  69.5 0.5 copy.101
  70.3 15.2 %all_gather.7 = bf16[32,48,48]{2,0,1:T(8,128)(2,1)S(1)} all-gather(bf16[32,12,48]{2,0,1:T(8,128)(2,1)S(1)} %copy.102), channel_id=1, replica_groups=mesh['groups'=2,'rows'=4,'chan'=2,'sub'=2] {'rows'}, dimensions={1}, use_global_device_ids=true | all-gather | bytes 184320 | tf_op jit(solution)/shard_map/all_gather | solution.py:67
  86.8 0.8 reshape.112
  87.6 3.4 %all-to-all-start.6 = ((bf16[4,2,2304]{2,1,0:T(2,128)(2,1)}), bf16[4,2,2304]{2,1,0:T(2,128)(2,1)S(1)}, u32[]{:S(2)}, u32[]{:S(2)}) async-start(bf16[4,2,2304]{2,1,0:T(2,128)(2,1)} %reshape.112), calls=%async_computation.6 | async-start | bytes 73728 | tf_op jit(solution)/shard_map/all_to_all | solution.py:70
  91.3 3.7 %all-to-all-done.6 = bf16[4,2,2304]{2,1,0:T(2,128)(2,1)S(1)} async-done(((bf16[4,2,2304]{2,1,0:T(2,128)(2,1)}), bf16[4,2,2304]{2,1,0:T(2,128)(2,1)S(1)}, u32[]{:S(2)}, u32[]{:S(2)}) %all-to-all-start.6) | async-done | bytes 36896 | tf_op jit(solution)/shard_map/all_to_all | solution.py:70
  96.2 0.5 copy-done.4
  96.7 0.9 fusion.10
  (69 shorter events, 10.4 us)
Async XLA Ops:
  0.0 1.2 %copy-start = (bf16[128,512]{1,0:T(8,128)(2,1)S(1)}, bf16[128,512]{1,0:T(8,128)(2,1)}, u32[]{:S(2)}) copy-start(bf16[128,512]{1,0:T(8,128)(2,1)} %param.10) | copy-start | bytes 393220
  0.0 1.0 %copy-start.1 = (bf16[12,12,128]{2,1,0:T(8,128)(2,1)S(1)}, bf16[12,12,128]{2,1,0:T(8,128)(2,1)}, u32[]{:S(2)}) copy-start(bf16[12,12,128]{2,1,0:T(8,128)(2,1)} %param.8) | copy-start | bytes 110596
  1.2 0.7 copy-start.5
  3.7 8.2 %all-to-all-start = ((bf16[4,2,2304]{2,1,0:T(2,128)(2,1)}), bf16[4,2,2304]{2,1,0:T(2,128)(2,1)S(1)}, u32[]{:S(2)}, u32[]{:S(2)}) async-start(bf16[4,2,2304]{2,1,0:T(2,128)(2,1)} %reshape.100), calls=%async_computation | async-start | bytes 73728 | tf_op jit(solution)/shard_map/all_to_all | solution.py:47
  11.9 7.2 %all-to-all-start.1 = ((bf16[4,2,2304]{2,1,0:T(2,128)(2,1)}), bf16[4,2,2304]{2,1,0:T(2,128)(2,1)S(1)}, u32[]{:S(2)}, u32[]{:S(2)}) async-start(bf16[4,2,2304]{2,1,0:T(2,128)(2,1)} %reshape.102), calls=%async_computation.1 | async-start | bytes 73728 | tf_op jit(solution)/shard_map/all_to_all | solution.py:48
  37.1 3.4 %copy-start.6 = (bf16[128,128]{1,0:T(8,128)(2,1)S(1)}, bf16[128,128]{1,0:T(8,128)(2,1)}, u32[]{:S(2)}) copy-start(bf16[128,128]{1,0:T(8,128)(2,1)} %param.11) | copy-start | bytes 98308
  37.1 7.3 %all-to-all-start.2 = ((bf16[4,2,2304]{2,1,0:T(2,128)(2,1)}), bf16[4,2,2304]{2,1,0:T(2,128)(2,1)S(1)}, u32[]{:S(2)}, u32[]{:S(2)}) async-start(bf16[4,2,2304]{2,1,0:T(2,128)(2,1)} %reshape.104), calls=%async_computation.2 | async-start | bytes 73728 | tf_op jit(solution)/shard_map/all_to_all | solution.py:56
  45.4 0.8 copy-start.3
  46.4 0.9 copy-start.2
  49.3 7.2 %all-to-all-start.3 = ((bf16[4,2,2304]{2,1,0:T(2,128)(2,1)}), bf16[4,2,2304]{2,1,0:T(2,128)(2,1)S(1)}, u32[]{:S(2)}, u32[]{:S(2)}) async-start(bf16[4,2,2304]{2,1,0:T(2,128)(2,1)} %reshape.106), calls=%async_computation.3 | async-start | bytes 73728 | tf_op jit(solution)/shard_map/all_to_all | solution.py:60
  56.5 7.2 %all-to-all-start.5 = ((bf16[4,2,2304]{2,1,0:T(2,128)(2,1)}), bf16[4,2,2304]{2,1,0:T(2,128)(2,1)S(1)}, u32[]{:S(2)}, u32[]{:S(2)}) async-start(bf16[4,2,2304]{2,1,0:T(2,128)(2,1)} %reshape.110), calls=%async_computation.5 | async-start | bytes 73728 | tf_op jit(solution)/shard_map/all_to_all | solution.py:61
  63.7 21.8 %all-to-all-start.4 = ((bf16[4,2,2304]{2,1,0:T(2,128)(2,1)}), bf16[4,2,2304]{2,1,0:T(2,128)(2,1)S(1)}, u32[]{:S(2)}, u32[]{:S(2)}) async-start(bf16[4,2,2304]{2,1,0:T(2,128)(2,1)} %reshape.108), calls=%async_computation.4 | async-start | bytes 73728 | tf_op jit(solution)/shard_map/all_to_all | solution.py:63
  87.6 3.4 %copy-start.7 = (bf16[128,128]{1,0:T(8,128)(2,1)S(1)}, bf16[128,128]{1,0:T(8,128)(2,1)}, u32[]{:S(2)}) copy-start(bf16[128,128]{1,0:T(8,128)(2,1)} %param.14) | copy-start | bytes 98308
  87.6 7.3 %all-to-all-start.6 = ((bf16[4,2,2304]{2,1,0:T(2,128)(2,1)}), bf16[4,2,2304]{2,1,0:T(2,128)(2,1)S(1)}, u32[]{:S(2)}, u32[]{:S(2)}) async-start(bf16[4,2,2304]{2,1,0:T(2,128)(2,1)} %reshape.112), calls=%async_computation.6 | async-start | bytes 73728 | tf_op jit(solution)/shard_map/all_to_all | solution.py:70
  95.9 0.8 copy-start.4
where the time goes:
time: 98.5 us; the launch traced here: 97.5 us
  blocking collectives  30.6 us (31%)
  starting transfers between devices  26.2 us (27%)
  local copies, waits for them, and re-layouts  18.4 us (19%)
  waiting for transfers between devices  16.8 us (17%)
  matrix products  2.72 us (3%)
  other arithmetic  2.31 us (2%)
    all_gather x2, blocking collectives, on_device(): lax.all_gather(right_grp, 'rows', axis=1, tiled=True)  30.6 us
    unnamed x30, local copies, waits for them, and re-layouts  11.3 us
    all_to_all x2, starting transfers between devices, on_device(): lax.all_to_all(left, ('chan', 'sub'), split_axis=0, concat_axis=2, tiled=...  7.47 us
    all_to_all x2, waiting for transfers between devices, on_device(): lax.all_to_all(tri, ('chan', 'sub'), split_axis=2, concat_axis=0, tiled=T...  7.34 us
    all_to_all x2, starting transfers between devices, on_device(): lax.all_to_all(tri, ('chan', 'sub'), split_axis=2, concat_axis=0, tiled=T...  6.8 us
    all_to_all x2, starting transfers between devices, on_device(): lax.all_to_all(right, ('chan', 'sub'), split_axis=0, concat_axis=2, tiled...  6.53 us
    all_to_all x1, starting transfers between devices, on_device(): lax.all_to_all(left_grp, 'rows', split_axis=2, concat_axis=1, tiled=True)  5.37 us
    all_to_all x2, waiting for transfers between devices, on_device(): lax.all_to_all(left, ('chan', 'sub'), split_axis=0, concat_axis=2, tiled=...  4.77 us
  transfers between devices with their start and end apart: 7, of which 6 were waited for; matrix products, arithmetic and copies ran while one was open for 8% of the time, Pallas kernels for 0%

commit v1 on v0

--- a/solution.py
+++ b/solution.py
@@ -1,6 +1,10 @@
+import functools
+
 import jax
 import jax.numpy as jnp
 from jax import lax
+from jax.experimental import pallas as pl
+from jax.experimental.pallas import tpu as pltpu
 from jax.sharding import PartitionSpec as P
 
 
@@ -71,9 +75,289 @@
     return finish(mid_f, tri_local, gate, in_proj)
 
 
+MESH = pl.DeviceIdType.MESH
+
+
+def sigmoid(x):
+    return 0.5 * jnp.tanh(0.5 * x) + 0.5
+
+
+def dot(x, y):
+    return jnp.dot(x, y, preferred_element_type=jnp.float32)
+
+
+def selection(shape, wide, narrow, turned):
+    dense_axis = 0 if shape[0] == narrow * narrow else 1
+    dense = lax.broadcasted_iota(jnp.int32, shape, dense_axis)
+    padded = lax.broadcasted_iota(jnp.int32, shape, 1 - dense_axis)
+    p, q = dense // narrow, dense % narrow
+    place = q * wide + p if turned else p * wide + q
+    return jnp.where(place == padded, 1.0, 0.0).astype(jnp.bfloat16)
+
+
+def kernel(
+    n,
+    side,
+    wide,
+    pair_hbm,
+    mask_ref,
+    w_ab1_hbm,
+    w_gate1_hbm,
+    w_proj1_hbm,
+    w_ab2_hbm,
+    w_gate2_hbm,
+    w_proj2_hbm,
+    out_ref,
+    pair_v,
+    w_ab1,
+    w_gate1,
+    w_proj1,
+    w_ab2,
+    w_gate2,
+    w_proj2,
+    padded,
+    left_wide,
+    right_wide,
+    a1,
+    b1,
+    b1_own,
+    a2,
+    a2_own,
+    b2,
+    in_sem,
+    a1_send,
+    a1_recv,
+    b1_send,
+    b1_recv,
+    a2_send,
+    a2_recv,
+    b2_send,
+    b2_recv,
+):
+    row = lax.axis_index("rows")
+    subs = lax.axis_size("sub")
+    col = lax.axis_index("chan") * subs + lax.axis_index("sub")
+
+    def device(r, c):
+        return {"rows": r, "chan": c // subs, "sub": c % subs}
+
+    loads = []
+    for place, (src, dst) in enumerate(
+        (
+            (pair_hbm, pair_v),
+            (w_ab1_hbm, w_ab1),
+            (w_gate1_hbm, w_gate1),
+            (w_proj1_hbm, w_proj1),
+            (w_ab2_hbm, w_ab2),
+            (w_gate2_hbm, w_gate2),
+            (w_proj2_hbm, w_proj2),
+        )
+    ):
+        load = pltpu.make_async_copy(src, dst, in_sem.at[place])
+        load.start()
+        loads.append(load)
+
+    barrier = pltpu.get_barrier_semaphore()
+    for step in range(1, n * n):
+        other = (row * n + col + step) % (n * n)
+        pl.semaphore_signal(
+            barrier, inc=1, device_id=device(other // n, other % n), device_id_type=MESH
+        )
+
+    squeeze = selection((side * side, side * wide), wide, side, False)
+    squeeze_turned = selection((side * side, side * wide), wide, side, True)
+    spread = selection((side * wide, side * side), wide, side, False)
+
+    sublane = lax.broadcasted_iota(jnp.int32, (wide, pair_hbm.shape[-1]), 0)
+    col_mask = jnp.zeros((wide, pair_hbm.shape[-1]), jnp.float32)
+    for j in range(side):
+        value = mask_ref[col * side + j].astype(jnp.float32)
+        col_mask = jnp.where(sublane == j, value, col_mask)
+    pair_mask = jnp.concatenate(
+        [col_mask * mask_ref[row * side + i].astype(jnp.float32) for i in range(side)], axis=0
+    )
+
+    padded[...] = jnp.zeros_like(padded)
+    loads[0].wait()
+    padded[:, :side, :] = pair_v[...].astype(jnp.float32)
+    pair_f = padded[...].reshape(side * wide, -1)
+
+    def prepare(values, w_ab, w_gate, load_ab, load_gate):
+        normed = normalize(values, -1).astype(jnp.bfloat16)
+        load_ab.wait()
+        proj = dot(normed, w_ab[...])
+        hidden = w_ab.shape[1] // 4
+        left = sigmoid(proj[:, :hidden]) * proj[:, hidden : 2 * hidden] * pair_mask
+        right = sigmoid(proj[:, 2 * hidden : 3 * hidden]) * proj[:, 3 * hidden :] * pair_mask
+
+        def gate():
+            load_gate.wait()
+            return sigmoid(dot(normed, w_gate[...]))
+
+        return left.astype(jnp.bfloat16), right.astype(jnp.bfloat16), gate
+
+    def finish(values, tri, gate, w_proj):
+        tri = tri.astype(jnp.bfloat16).astype(jnp.float32)
+        tnorm = normalize(tri, -1).astype(jnp.bfloat16)
+        return (values + gate * dot(tnorm, w_proj[...])).astype(jnp.bfloat16)
+
+    def send(src, buf, slot, send_sem, recv_sem, r, c):
+        return pltpu.make_async_remote_copy(
+            src_ref=src,
+            dst_ref=buf.at[slot],
+            send_sem=send_sem,
+            recv_sem=recv_sem.at[slot],
+            device_id=device(r, c),
+            device_id_type=MESH,
+        )
+
+    def await_block(buf, slot, send_sem, recv_sem):
+        send(buf.at[slot], buf, slot, send_sem, recv_sem, row, col).wait_recv()
+
+    def add_products(total, left, right):
+        left_wide[...] = dot(spread, left[...]).reshape(left_wide.shape)
+        right_wide[...] = dot(spread, right[...]).reshape(right_wide.shape)
+
+        def step(k, total):
+            row_of_right = right_wide[k]
+            return tuple(
+                total[i] + left_wide[k, pl.ds(i, 1), :] * row_of_right for i in range(side)
+            )
+
+        return lax.fori_loop(0, side, step, total, unroll=True)
+
+    def zeros():
+        return tuple(
+            jnp.zeros((wide, pair_hbm.shape[-1]), jnp.float32) for _ in range(side)
+        )
+
+    left, right, gate = prepare(pair_f, w_ab1, w_gate1, loads[1], loads[2])
+    a1[col] = dot(squeeze_turned, left).astype(jnp.bfloat16)
+    b1_own[...] = dot(squeeze_turned, right).astype(jnp.bfloat16)
+    pl.semaphore_wait(barrier, n * n - 1)
+    mine = row == col
+    sends = []
+    for s in range(1, n):
+        copy = send(b1_own, b1, col, b1_send.at[s], b1_recv, (row + s) % n, row)
+        copy.start()
+        sends.append(copy)
+    turn1 = send(b1_own, b1, col, b1_send.at[0], b1_recv, row, row)
+
+    @pl.when(jnp.logical_not(mine))
+    def _():
+        turn1.start()
+
+    for s in range(1, n):
+        copy = send(a1.at[col], a1, col, a1_send.at[s], a1_recv, row, (col + s) % n)
+        copy.start()
+        sends.append(copy)
+
+    @pl.when(mine)
+    def _():
+        b1[col] = b1_own[...]
+
+    gate1 = gate()
+    total = zeros()
+    for s in range(n):
+        block = (col + s) % n
+        if s:
+            await_block(a1, block, a1_send.at[0], a1_recv)
+            await_block(b1, block, b1_send.at[0], b1_recv)
+        else:
+
+            @pl.when(jnp.logical_not(mine))
+            def _():
+                await_block(b1, block, b1_send.at[0], b1_recv)
+
+        total = add_products(total, a1.at[block], b1.at[block])
+    loads[3].wait()
+    middle = finish(pair_f, jnp.concatenate(total, axis=0), gate1, w_proj1)
+
+    mid_f = middle.astype(jnp.float32)
+    left, right, gate = prepare(mid_f, w_ab2, w_gate2, loads[4], loads[5])
+    b2[row] = dot(squeeze, right).astype(jnp.bfloat16)
+    a2_own[...] = dot(squeeze, left).astype(jnp.bfloat16)
+    for s in range(1, n):
+        copy = send(b2.at[row], b2, row, b2_send.at[s], b2_recv, (row + s) % n, col)
+        copy.start()
+        sends.append(copy)
+    for s in range(1, n):
+        copy = send(a2_own, a2, row, a2_send.at[s], a2_recv, col, (col + s) % n)
+        copy.start()
+        sends.append(copy)
+    turn2 = send(a2_own, a2, row, a2_send.at[0], a2_recv, col, col)
+
+    @pl.when(jnp.logical_not(mine))
+    def _():
+        turn2.start()
+
+    @pl.when(mine)
+    def _():
+        a2[row] = a2_own[...]
+
+    gate2 = gate()
+    total = zeros()
+    for s in range(n):
+        block = (row + s) % n
+        if s:
+            await_block(a2, block, a2_send.at[0], a2_recv)
+            await_block(b2, block, b2_send.at[0], b2_recv)
+        else:
+
+            @pl.when(jnp.logical_not(mine))
+            def _():
+                await_block(a2, block, a2_send.at[0], a2_recv)
+
+        total = add_products(total, a2.at[block], b2.at[block])
+    loads[6].wait()
+    updated = finish(mid_f, jnp.concatenate(total, axis=0), gate2, w_proj2)
+    out_ref[...] = updated.reshape(side, wide, -1)[:, :side, :]
+    for copy in sends:
+        copy.wait_send()
+
+    @pl.when(jnp.logical_not(mine))
+    def _():
+        turn1.wait_send()
+        turn2.wait_send()
+
+
+def on_square(n, pair, res_mask, *weights):
+    side, _, channels = pair.shape
+    wide = -(-side // 16) * 16
+    block = (side * side, channels)
+    blocks = pltpu.VMEM((n, *block), jnp.bfloat16)
+    spread_out = pltpu.VMEM((side, wide, channels), jnp.float32)
+    sems = pltpu.SemaphoreType.DMA((n,))
+    anywhere = pl.BlockSpec(memory_space=pl.ANY)
+    return pl.pallas_call(
+        functools.partial(kernel, n, side, wide),
+        out_shape=jax.ShapeDtypeStruct(pair.shape, pair.dtype),
+        in_specs=[anywhere, pl.BlockSpec(memory_space=pltpu.SMEM)] + [anywhere] * len(weights),
+        out_specs=pl.BlockSpec(memory_space=pltpu.VMEM),
+        scratch_shapes=[pltpu.VMEM(pair.shape, pair.dtype)]
+        + [pltpu.VMEM(w.shape, w.dtype) for w in weights]
+        + [spread_out] * 3
+        + [blocks, blocks, pltpu.VMEM(block, jnp.bfloat16)]
+        + [blocks, pltpu.VMEM(block, jnp.bfloat16), blocks]
+        + [pltpu.SemaphoreType.DMA((1 + len(weights),))]
+        + [sems] * 8,
+        compiler_params=pltpu.CompilerParams(
+            collective_id=0, has_side_effects=True, vmem_limit_bytes=32 * 2**20
+        ),
+    )(pair, res_mask, *weights)
+
+
 def solution(mesh):
+    n = mesh.shape["rows"]
+    square = n == mesh.shape["chan"] * mesh.shape["sub"]
+
+    def per_device(pair, *rest):
+        if square and pair.shape[0] == pair.shape[1] and pair.shape[0] <= 16:
+            return on_square(n, pair, *rest)
+        return on_device(pair, *rest)
+
     return jax.shard_map(
-        on_device,
+        per_device,
         mesh=mesh,
         in_specs=(
             P(("groups", "rows"), ("chan", "sub"), None),

time: 98.5 us -> 32.8 us (0.33)
  blocking collectives: 30.6 us -> 0 us
  starting transfers between devices: 26.2 us -> 0 us
  Pallas kernels: 0 us -> 25.4 us
  waiting for transfers between devices: 16.8 us -> 0 us
  local copies, waits for them, and re-layouts: 18.4 us -> 6.91 us
  matrix products: 2.72 us -> 0 us
  other arithmetic: 2.31 us -> 0 us
    all_gather x2 -> x0, blocking collectives: 30.6 us -> none  [on_device(): lax.all_gather(right_grp, 'rows', axis=1, tiled=True)]
    all_to_all x7 -> x0, starting transfers between devices: 26.2 us -> none  [the longest x2 7.47 us: on_device(): lax.all_to_all(left, ('chan', 'sub'), split_axis=0, concat_axis=2, tiled=...]
    pallas_call x0 -> x1, Pallas kernels: none -> 25.4 us  [on_square(): pl.pallas_call(functools.partial(kernel, n, side, wide), out_shape=jax.Sh...]
    all_to_all x7 -> x0, waiting for transfers between devices: 16.8 us -> none  [the longest x2 7.34 us: on_device(): lax.all_to_all(tri, ('chan', 'sub'), split_axis=2, concat_axis=0, tiled=T...]
    unnamed x30 -> x17, local copies, waits for them, and re-layouts: 11.3 us -> 6.91 us
    all_to_all x14 -> x0, local copies, waits for them, and re-layouts: 3.89 us -> none  [the longest x6 1.45 us: on_device(): lax.all_to_all(right, ('chan', 'sub'), split_axis=0, concat_axis=2, tiled...]
    convert_element_type x14 -> x0, local copies, waits for them, and re-layouts: 3.19 us -> none  [the longest x2 0.91 us: prepare(): (jax.nn.sigmoid(proj[:hidden]) * proj[hidden:2 * hidden] * pair_mask).ast...]
    dot_general x8 -> x0, matrix products: 2.72 us -> none  [the longest x2 1.16 us: finish(): jnp.einsum('dij,de->ije', tnorm, w_proj, preferred_element_type=jnp.float32)]
  transfers between devices with their start and end apart: 7 -> 0, of which waited for: 6 -> 0; matrix products, arithmetic and copies ran while one was open for 8% -> 0% of each run, Pallas kernels for 0% -> 0%
where the time goes in v1:
time: 32.8 us; the launch traced here: 32.4 us
  Pallas kernels  25.4 us (77%)
  local copies, waits for them, and re-layouts  6.91 us (21%)
    pallas_call x1, Pallas kernels, on_square(): pl.pallas_call(functools.partial(kernel, n, side, wide), out_shape=jax.Sh...  25.4 us
    unnamed x17, local copies, waits for them, and re-layouts  6.91 us

profile of v1, /device:TPU:0, one launch (start us, length us, event | category | flops | bytes accessed | tf_op | source)
XLA Modules:
  0.0 32.4 jit_solution(3118069985111174696)
XLA Ops:
  0.0 0.0 copy-start
  0.0 0.9 %copy-done = bf16[128,512]{1,0:T(8,128)(2,1)S(1)} copy-done((bf16[128,512]{1,0:T(8,128)(2,1)S(1)}, bf16[128,512]{1,0:T(8,128)(2,1)}, u32[]{:S(2)}) %copy-start) | copy-done | bytes 131096
  0.9 0.0 copy-start.1
  0.9 0.9 %copy-done.1 = bf16[128,512]{1,0:T(8,128)(2,1)S(1)} copy-done((bf16[128,512]{1,0:T(8,128)(2,1)S(1)}, bf16[128,512]{1,0:T(8,128)(2,1)}, u32[]{:S(2)}) %copy-start.1) | copy-done | bytes 131096
  1.8 0.0 copy-start.2
  1.8 0.8 %copy-done.2 = bf16[12,12,128]{2,1,0:T(8,128)(2,1)S(1)} copy-done((bf16[12,12,128]{2,1,0:T(8,128)(2,1)S(1)}, bf16[12,12,128]{2,1,0:T(8,128)(2,1)}, u32[]{:S(2)}) %copy-start.2) | copy-done | bytes 36888
  2.6 0.0 copy-start.3
  2.6 0.8 %copy-done.3 = bf16[128,128]{1,0:T(8,128)(2,1)S(1)} copy-done((bf16[128,128]{1,0:T(8,128)(2,1)S(1)}, bf16[128,128]{1,0:T(8,128)(2,1)}, u32[]{:S(2)}) %copy-start.3) | copy-done | bytes 32792
  3.4 0.0 copy-start.4
  3.4 0.8 %copy-done.4 = bf16[128,128]{1,0:T(8,128)(2,1)S(1)} copy-done((bf16[128,128]{1,0:T(8,128)(2,1)S(1)}, bf16[128,128]{1,0:T(8,128)(2,1)}, u32[]{:S(2)}) %copy-start.4) | copy-done | bytes 32792
  4.1 0.0 copy-start.5
  4.1 0.8 %copy-done.5 = bf16[128,128]{1,0:T(8,128)(2,1)S(1)} copy-done((bf16[128,128]{1,0:T(8,128)(2,1)S(1)}, bf16[128,128]{1,0:T(8,128)(2,1)}, u32[]{:S(2)}) %copy-start.5) | copy-done | bytes 32792
  4.9 0.0 copy-start.6
  4.9 0.8 %copy-done.6 = bf16[128,128]{1,0:T(8,128)(2,1)S(1)} copy-done((bf16[128,128]{1,0:T(8,128)(2,1)S(1)}, bf16[128,128]{1,0:T(8,128)(2,1)}, u32[]{:S(2)}) %copy-start.6) | copy-done | bytes 32792
  5.6 0.0 copy-start.7
  5.6 0.7 %copy-done.7 = s32[48]{0:T(128)S(1)} copy-done((s32[48]{0:T(128)S(1)}, s32[48]{0:T(128)}, u32[]{:S(2)}) %copy-start.7) | copy-done | bytes 216
  6.3 25.4 %shard_map.82 = bf16[12,12,128]{2,1,0:T(8,128)(2,1)S(1)} custom-call(bf16[12,12,128]{2,1,0:T(8,128)(2,1)S(1)} %copy-done.2, s32[48]{0:T(128)S(1)} %copy-done.7, bf16[128,512]{1,0:T(8,128)(2,1)S(1)} %copy-done, bf16[128,128]{1,0:T(8,128)(2,1)S(1)} %copy-done.3, bf16[128,128]{1,0:T(8,128)(2,1)S(1)} %copy-done.4, bf16[128,512]{1,0:T(8,128)(2,1)S(1)} %copy-done.1, ...), custom_call_target="tpu_custom_call" | custom-call | tf_op jit(solution)/shard_map/pallas_call | solution.py:332
  31.7 0.6 %copy.10 = bf16[12,12,128]{2,1,0:T(8,128)(2,1)} copy(bf16[12,12,128]{2,1,0:T(8,128)(2,1)S(1)} %shard_map.82) | data formatting | bytes 73728
Async XLA Ops:
  0.0 0.9 %copy-start = (bf16[128,512]{1,0:T(8,128)(2,1)S(1)}, bf16[128,512]{1,0:T(8,128)(2,1)}, u32[]{:S(2)}) copy-start(bf16[128,512]{1,0:T(8,128)(2,1)} %w_ab1_hbm.1) | copy-start | bytes 393220
  0.9 0.9 %copy-start.1 = (bf16[128,512]{1,0:T(8,128)(2,1)S(1)}, bf16[128,512]{1,0:T(8,128)(2,1)}, u32[]{:S(2)}) copy-start(bf16[128,512]{1,0:T(8,128)(2,1)} %w_ab2_hbm.1) | copy-start | bytes 393220
  1.8 0.8 %copy-start.2 = (bf16[12,12,128]{2,1,0:T(8,128)(2,1)S(1)}, bf16[12,12,128]{2,1,0:T(8,128)(2,1)}, u32[]{:S(2)}) copy-start(bf16[12,12,128]{2,1,0:T(8,128)(2,1)} %pair_hbm.1) | copy-start | bytes 110596
  2.6 0.8 %copy-start.3 = (bf16[128,128]{1,0:T(8,128)(2,1)S(1)}, bf16[128,128]{1,0:T(8,128)(2,1)}, u32[]{:S(2)}) copy-start(bf16[128,128]{1,0:T(8,128)(2,1)} %w_gate1_hbm.1) | copy-start | bytes 98308
  3.4 0.8 %copy-start.4 = (bf16[128,128]{1,0:T(8,128)(2,1)S(1)}, bf16[128,128]{1,0:T(8,128)(2,1)}, u32[]{:S(2)}) copy-start(bf16[128,128]{1,0:T(8,128)(2,1)} %w_proj1_hbm.1) | copy-start | bytes 98308
  4.1 0.8 %copy-start.5 = (bf16[128,128]{1,0:T(8,128)(2,1)S(1)}, bf16[128,128]{1,0:T(8,128)(2,1)}, u32[]{:S(2)}) copy-start(bf16[128,128]{1,0:T(8,128)(2,1)} %w_gate2_hbm.1) | copy-start | bytes 98308
  4.9 0.8 %copy-start.6 = (bf16[128,128]{1,0:T(8,128)(2,1)S(1)}, bf16[128,128]{1,0:T(8,128)(2,1)}, u32[]{:S(2)}) copy-start(bf16[128,128]{1,0:T(8,128)(2,1)} %w_proj2_hbm.1) | copy-start | bytes 98308
  5.6 0.7 %copy-start.7 = (s32[48]{0:T(128)S(1)}, s32[48]{0:T(128)}, u32[]{:S(2)}) copy-start(s32[48]{0:T(128)} %mask_ref.1) | copy-start | bytes 580

commit v2 on v1

--- a/solution.py
+++ b/solution.py
@@ -100,7 +100,7 @@
     side,
     wide,
     pair_hbm,
-    mask_ref,
+    mask_hbm,
     w_ab1_hbm,
     w_gate1_hbm,
     w_proj1_hbm,
@@ -109,6 +109,7 @@
     w_proj2_hbm,
     out_ref,
     pair_v,
+    mask_ref,
     w_ab1,
     w_gate1,
     w_proj1,
@@ -145,6 +146,7 @@
     for place, (src, dst) in enumerate(
         (
             (pair_hbm, pair_v),
+            (mask_hbm, mask_ref),
             (w_ab1_hbm, w_ab1),
             (w_gate1_hbm, w_gate1),
             (w_proj1_hbm, w_proj1),
@@ -168,6 +170,7 @@
     squeeze_turned = selection((side * side, side * wide), wide, side, True)
     spread = selection((side * wide, side * side), wide, side, False)
 
+    loads[1].wait()
     sublane = lax.broadcasted_iota(jnp.int32, (wide, pair_hbm.shape[-1]), 0)
     col_mask = jnp.zeros((wide, pair_hbm.shape[-1]), jnp.float32)
     for j in range(side):
@@ -231,7 +234,7 @@
             jnp.zeros((wide, pair_hbm.shape[-1]), jnp.float32) for _ in range(side)
         )
 
-    left, right, gate = prepare(pair_f, w_ab1, w_gate1, loads[1], loads[2])
+    left, right, gate = prepare(pair_f, w_ab1, w_gate1, loads[2], loads[3])
     a1[col] = dot(squeeze_turned, left).astype(jnp.bfloat16)
     b1_own[...] = dot(squeeze_turned, right).astype(jnp.bfloat16)
     pl.semaphore_wait(barrier, n * n - 1)
@@ -270,11 +273,11 @@
                 await_block(b1, block, b1_send.at[0], b1_recv)
 
         total = add_products(total, a1.at[block], b1.at[block])
-    loads[3].wait()
+    loads[4].wait()
     middle = finish(pair_f, jnp.concatenate(total, axis=0), gate1, w_proj1)
 
     mid_f = middle.astype(jnp.float32)
-    left, right, gate = prepare(mid_f, w_ab2, w_gate2, loads[4], loads[5])
+    left, right, gate = prepare(mid_f, w_ab2, w_gate2, loads[5], loads[6])
     b2[row] = dot(squeeze, right).astype(jnp.bfloat16)
     a2_own[...] = dot(squeeze, left).astype(jnp.bfloat16)
     for s in range(1, n):
@@ -309,7 +312,7 @@
                 await_block(a2, block, a2_send.at[0], a2_recv)
 
         total = add_products(total, a2.at[block], b2.at[block])
-    loads[6].wait()
+    loads[7].wait()
     updated = finish(mid_f, jnp.concatenate(total, axis=0), gate2, w_proj2)
     out_ref[...] = updated.reshape(side, wide, -1)[:, :side, :]
     for copy in sends:
@@ -328,21 +331,22 @@
     blocks = pltpu.VMEM((n, *block), jnp.bfloat16)
     spread_out = pltpu.VMEM((side, wide, channels), jnp.float32)
     sems = pltpu.SemaphoreType.DMA((n,))
-    anywhere = pl.BlockSpec(memory_space=pl.ANY)
+    in_hbm = pl.BlockSpec(memory_space=pltpu.HBM)
     return pl.pallas_call(
         functools.partial(kernel, n, side, wide),
         out_shape=jax.ShapeDtypeStruct(pair.shape, pair.dtype),
-        in_specs=[anywhere, pl.BlockSpec(memory_space=pltpu.SMEM)] + [anywhere] * len(weights),
+        in_specs=[in_hbm] * (2 + len(weights)),
         out_specs=pl.BlockSpec(memory_space=pltpu.VMEM),
         scratch_shapes=[pltpu.VMEM(pair.shape, pair.dtype)]
+        + [pltpu.SMEM(res_mask.shape, res_mask.dtype)]
         + [pltpu.VMEM(w.shape, w.dtype) for w in weights]
         + [spread_out] * 3
         + [blocks, blocks, pltpu.VMEM(block, jnp.bfloat16)]
         + [blocks, pltpu.VMEM(block, jnp.bfloat16), blocks]
-        + [pltpu.SemaphoreType.DMA((1 + len(weights),))]
+        + [pltpu.SemaphoreType.DMA((2 + len(weights),))]
         + [sems] * 8,
         compiler_params=pltpu.CompilerParams(
-            collective_id=0, has_side_effects=True, vmem_limit_bytes=32 * 2**20
+            collective_id=0, has_side_effects=True, vmem_limit_bytes=60 * 2**20
         ),
     )(pair, res_mask, *weights)
 

time: 32.8 us -> 26.5 us (0.81)
  local copies, waits for them, and re-layouts: 6.91 us -> 1.42 us
  Pallas kernels: 25.4 us -> 24.9 us
    unnamed x17 -> x1, local copies, waits for them, and re-layouts: 6.91 us -> 1.42 us
    pallas_call x1, Pallas kernels: 25.4 us -> 24.9 us  [on_square(): pl.pallas_call(functools.partial(kernel, n, side, wide), out_shape=jax.Sh...]
where the time goes in v2:
time: 26.5 us; the launch traced here: 26.4 us
  Pallas kernels  24.9 us (94%)
  local copies, waits for them, and re-layouts  1.42 us (5%)
    pallas_call x1, Pallas kernels, on_square(): pl.pallas_call(functools.partial(kernel, n, side, wide), out_shape=jax.Sh...  24.9 us
    unnamed x1, local copies, waits for them, and re-layouts  1.42 us

profile of v2, /device:TPU:0, one launch (start us, length us, event | category | flops | bytes accessed | tf_op | source)
XLA Modules:
  0.0 26.4 jit_solution(16034372771747482177)
XLA Ops:
  0.0 24.9 %shard_map.82 = bf16[12,12,128]{2,1,0:T(8,128)(2,1)} custom-call(bf16[12,12,128]{2,1,0:T(8,128)(2,1)} %pair_hbm.1, s32[48]{0:T(128)} %mask_hbm.1, bf16[128,512]{1,0:T(8,128)(2,1)} %w_ab1_hbm.1, bf16[128,128]{1,0:T(8,128)(2,1)} %w_gate1_hbm.1, bf16[128,128]{1,0:T(8,128)(2,1)} %w_proj1_hbm.1, bf16[128,512]{1,0:T(8,128)(2,1)} %w_ab2_hbm.1, ...), custom_call_target="tpu_custom_call" | custom-call | tf_op jit(solution)/shard_map/pallas_call | solution.py:335
  24.9 1.4 %copy.10 = bf16[12,12,128]{2,1,0:T(8,128)(2,1)} copy(bf16[12,12,128]{2,1,0:T(8,128)(2,1)} %shard_map.82) | data formatting | bytes 73728

commit v3 on v2

--- a/solution.py
+++ b/solution.py
@@ -119,13 +119,18 @@
     padded,
     left_wide,
     right_wide,
+    pair_t,
     a1,
+    a1_own,
     b1,
-    b1_own,
+    mid_t,
+    mid_own,
     a2,
-    a2_own,
     b2,
+    b2_own,
     in_sem,
+    t_send,
+    t_recv,
     a1_send,
     a1_recv,
     b1_send,
@@ -138,6 +143,8 @@
     row = lax.axis_index("rows")
     subs = lax.axis_size("sub")
     col = lax.axis_index("chan") * subs + lax.axis_index("sub")
+    mine = row == col
+    channels = pair_hbm.shape[-1]
 
     def device(r, c):
         return {"rows": r, "chan": c // subs, "sub": c % subs}
@@ -170,57 +177,66 @@
     squeeze_turned = selection((side * side, side * wide), wide, side, True)
     spread = selection((side * wide, side * side), wide, side, False)
 
-    loads[1].wait()
-    sublane = lax.broadcasted_iota(jnp.int32, (wide, pair_hbm.shape[-1]), 0)
-    col_mask = jnp.zeros((wide, pair_hbm.shape[-1]), jnp.float32)
-    for j in range(side):
-        value = mask_ref[col * side + j].astype(jnp.float32)
-        col_mask = jnp.where(sublane == j, value, col_mask)
-    pair_mask = jnp.concatenate(
-        [col_mask * mask_ref[row * side + i].astype(jnp.float32) for i in range(side)], axis=0
-    )
-
-    padded[...] = jnp.zeros_like(padded)
-    loads[0].wait()
-    padded[:, :side, :] = pair_v[...].astype(jnp.float32)
-    pair_f = padded[...].reshape(side * wide, -1)
-
-    def prepare(values, w_ab, w_gate, load_ab, load_gate):
-        normed = normalize(values, -1).astype(jnp.bfloat16)
-        load_ab.wait()
-        proj = dot(normed, w_ab[...])
+    def tile_mask(rows, cols):
+        sublane = lax.broadcasted_iota(jnp.int32, (wide, channels), 0)
+        col_mask = jnp.zeros((wide, channels), jnp.float32)
+        for j in range(side):
+            value = mask_ref[cols * side + j].astype(jnp.float32)
+            col_mask = jnp.where(sublane == j, value, col_mask)
+        return jnp.concatenate(
+            [col_mask * mask_ref[rows * side + i].astype(jnp.float32) for i in range(side)],
+            axis=0,
+        )
+
+    def widen(block):
+        padded[:, :side, :] = block[...].astype(jnp.float32)
+        return padded[...].reshape(side * wide, channels)
+
+    def norm(values):
+        return normalize(values, -1).astype(jnp.bfloat16)
+
+    def gated(normed, w_ab, half, mask):
         hidden = w_ab.shape[1] // 4
-        left = sigmoid(proj[:, :hidden]) * proj[:, hidden : 2 * hidden] * pair_mask
-        right = sigmoid(proj[:, 2 * hidden : 3 * hidden]) * proj[:, 3 * hidden :] * pair_mask
-
-        def gate():
-            load_gate.wait()
-            return sigmoid(dot(normed, w_gate[...]))
-
-        return left.astype(jnp.bfloat16), right.astype(jnp.bfloat16), gate
-
-    def finish(values, tri, gate, w_proj):
-        tri = tri.astype(jnp.bfloat16).astype(jnp.float32)
-        tnorm = normalize(tri, -1).astype(jnp.bfloat16)
-        return (values + gate * dot(tnorm, w_proj[...])).astype(jnp.bfloat16)
-
-    def send(src, buf, slot, send_sem, recv_sem, r, c):
+        proj = dot(normed, w_ab[:, 2 * half * hidden : 2 * (half + 1) * hidden])
+        return (sigmoid(proj[:, :hidden]) * proj[:, hidden:] * mask).astype(jnp.bfloat16)
+
+    def finish(values, total, gate, w_proj):
+        tri = jnp.concatenate(total, axis=0).astype(jnp.bfloat16).astype(jnp.float32)
+        return (values + gate * dot(norm(tri), w_proj[...])).astype(jnp.bfloat16)
+
+    def send(src, dst, send_sem, recv_sem, r, c):
         return pltpu.make_async_remote_copy(
             src_ref=src,
-            dst_ref=buf.at[slot],
+            dst_ref=dst,
             send_sem=send_sem,
-            recv_sem=recv_sem.at[slot],
+            recv_sem=recv_sem,
             device_id=device(r, c),
             device_id_type=MESH,
         )
 
-    def await_block(buf, slot, send_sem, recv_sem):
-        send(buf.at[slot], buf, slot, send_sem, recv_sem, row, col).wait_recv()
-
-    def add_products(total, left, right):
-        left_wide[...] = dot(spread, left[...]).reshape(left_wide.shape)
-        right_wide[...] = dot(spread, right[...]).reshape(right_wide.shape)
-
+    sends = []
+
+    def spread_out(along, along_buf, along_sems, turn, turn_buf, turn_sems):
+        for s in range(1, n):
+            copy = send(
+                turn, turn_buf.at[col], turn_sems[0].at[s], turn_sems[1].at[col], (col + s) % n, row
+            )
+            copy.start()
+            sends.append(copy)
+        for s in range(1, n):
+            copy = send(
+                along, along_buf.at[col], along_sems[0].at[s], along_sems[1].at[col], row, (col + s) % n
+            )
+            copy.start()
+            sends.append(copy)
+
+    def await_block(buf, slot, sems):
+        send(buf.at[slot], buf.at[slot], sems[0].at[0], sems[1].at[slot], row, col).wait_recv()
+
+    def widen_block(dst, block):
+        dst[...] = dot(spread, block[...]).reshape(dst.shape)
+
+    def add_products(total):
         def step(k, total):
             row_of_right = right_wide[k]
             return tuple(
@@ -230,106 +246,117 @@
         return lax.fori_loop(0, side, step, total, unroll=True)
 
     def zeros():
-        return tuple(
-            jnp.zeros((wide, pair_hbm.shape[-1]), jnp.float32) for _ in range(side)
-        )
-
-    left, right, gate = prepare(pair_f, w_ab1, w_gate1, loads[2], loads[3])
-    a1[col] = dot(squeeze_turned, left).astype(jnp.bfloat16)
-    b1_own[...] = dot(squeeze_turned, right).astype(jnp.bfloat16)
+        return tuple(jnp.zeros((wide, channels), jnp.float32) for _ in range(side))
+
+    def contract(along, along_wide, along_sems, turn, turn_wide, turn_sems):
+        total = zeros()
+        for s in range(n):
+            block = (row + s) % n
+            if s:
+                await_block(turn, block, turn_sems)
+                widen_block(turn_wide, turn.at[block])
+
+            @pl.when(block != col)
+            def _():
+                await_block(along, block, along_sems)
+
+            widen_block(along_wide, along.at[block])
+            total = add_products(total)
+        return total
+
+    a1_sems, b1_sems = (a1_send, a1_recv), (b1_send, b1_recv)
+    a2_sems, b2_sems = (a2_send, a2_recv), (b2_send, b2_recv)
+    padded[...] = jnp.zeros_like(padded)
+    loads[0].wait()
+    pair_f = widen(pair_v)
+    normed = norm(pair_f)
+    loads[1].wait()
+    mask = tile_mask(row, col)
+    mask_t = tile_mask(col, row)
+    loads[2].wait()
+    left = gated(normed, w_ab1, 0, mask)
+    right = gated(normed, w_ab1, 1, mask)
+    a1_own[...] = dot(squeeze_turned, left).astype(jnp.bfloat16)
+    b1[col] = dot(squeeze_turned, right).astype(jnp.bfloat16)
+
     pl.semaphore_wait(barrier, n * n - 1)
-    mine = row == col
-    sends = []
-    for s in range(1, n):
-        copy = send(b1_own, b1, col, b1_send.at[s], b1_recv, (row + s) % n, row)
-        copy.start()
-        sends.append(copy)
-    turn1 = send(b1_own, b1, col, b1_send.at[0], b1_recv, row, row)
+    turn_pair = send(pair_hbm, pair_t, t_send.at[0], t_recv.at[0], col, row)
+    stay_pair = pltpu.make_async_copy(pair_hbm, pair_t, t_send.at[0])
 
     @pl.when(jnp.logical_not(mine))
     def _():
-        turn1.start()
-
-    for s in range(1, n):
-        copy = send(a1.at[col], a1, col, a1_send.at[s], a1_recv, row, (col + s) % n)
-        copy.start()
-        sends.append(copy)
+        turn_pair.start()
 
     @pl.when(mine)
     def _():
-        b1[col] = b1_own[...]
-
-    gate1 = gate()
-    total = zeros()
-    for s in range(n):
-        block = (col + s) % n
-        if s:
-            await_block(a1, block, a1_send.at[0], a1_recv)
-            await_block(b1, block, b1_send.at[0], b1_recv)
-        else:
-
-            @pl.when(jnp.logical_not(mine))
-            def _():
-                await_block(b1, block, b1_send.at[0], b1_recv)
-
-        total = add_products(total, a1.at[block], b1.at[block])
+        stay_pair.start()
+
+    spread_out(b1.at[col], b1, b1_sems, a1_own, a1, a1_sems)
+
+    @pl.when(jnp.logical_not(mine))
+    def _():
+        turn_pair.wait_recv()
+
+    @pl.when(mine)
+    def _():
+        stay_pair.wait()
+
+    pair_f = widen(pair_t)
+    normed = norm(pair_f)
+    turned = dot(squeeze_turned, gated(normed, w_ab1, 0, mask_t)).astype(jnp.bfloat16)
+    left_wide[...] = dot(spread, turned).reshape(left_wide.shape)
+    loads[3].wait()
+    gate = sigmoid(dot(normed, w_gate1[...]))
+    total = contract(b1, right_wide, b1_sems, a1, left_wide, a1_sems)
     loads[4].wait()
-    middle = finish(pair_f, jnp.concatenate(total, axis=0), gate1, w_proj1)
-
-    mid_f = middle.astype(jnp.float32)
-    left, right, gate = prepare(mid_f, w_ab2, w_gate2, loads[5], loads[6])
-    b2[row] = dot(squeeze, right).astype(jnp.bfloat16)
-    a2_own[...] = dot(squeeze, left).astype(jnp.bfloat16)
-    for s in range(1, n):
-        copy = send(b2.at[row], b2, row, b2_send.at[s], b2_recv, (row + s) % n, col)
-        copy.start()
-        sends.append(copy)
-    for s in range(1, n):
-        copy = send(a2_own, a2, row, a2_send.at[s], a2_recv, col, (col + s) % n)
-        copy.start()
-        sends.append(copy)
-    turn2 = send(a2_own, a2, row, a2_send.at[0], a2_recv, col, col)
+    middle = finish(pair_f, total, gate, w_proj1)
+
+    mid_own[...] = dot(squeeze, middle).astype(jnp.bfloat16)
+    turn_mid = send(mid_own, mid_t, t_send.at[1], t_recv.at[1], col, row)
 
     @pl.when(jnp.logical_not(mine))
     def _():
-        turn2.start()
+        turn_mid.start()
+
+    normed = norm(middle.astype(jnp.float32))
+    loads[5].wait()
+    b2_own[...] = dot(squeeze, gated(normed, w_ab2, 1, mask_t)).astype(jnp.bfloat16)
+    a2[col] = dot(squeeze, gated(normed, w_ab2, 0, mask_t)).astype(jnp.bfloat16)
+    spread_out(a2.at[col], a2, a2_sems, b2_own, b2, b2_sems)
+
+    @pl.when(jnp.logical_not(mine))
+    def _():
+        turn_mid.wait_recv()
 
     @pl.when(mine)
     def _():
-        a2[row] = a2_own[...]
-
-    gate2 = gate()
-    total = zeros()
-    for s in range(n):
-        block = (row + s) % n
-        if s:
-            await_block(a2, block, a2_send.at[0], a2_recv)
-            await_block(b2, block, b2_send.at[0], b2_recv)
-        else:
-
-            @pl.when(jnp.logical_not(mine))
-            def _():
-                await_block(a2, block, a2_send.at[0], a2_recv)
-
-        total = add_products(total, a2.at[block], b2.at[block])
+        mid_t[...] = mid_own[...]
+
+    mid_f = dot(spread, mid_t[...])
+    normed = norm(mid_f)
+    right_wide[...] = gated(normed, w_ab2, 1, mask).astype(jnp.float32).reshape(right_wide.shape)
+    loads[6].wait()
+    gate = sigmoid(dot(normed, w_gate2[...]))
+    total = contract(a2, left_wide, a2_sems, b2, right_wide, b2_sems)
     loads[7].wait()
-    updated = finish(mid_f, jnp.concatenate(total, axis=0), gate2, w_proj2)
-    out_ref[...] = updated.reshape(side, wide, -1)[:, :side, :]
+    updated = finish(mid_f, total, gate, w_proj2)
+    out_ref[...] = updated.reshape(side, wide, channels)[:, :side, :]
     for copy in sends:
         copy.wait_send()
 
     @pl.when(jnp.logical_not(mine))
     def _():
-        turn1.wait_send()
-        turn2.wait_send()
+        turn_pair.wait_send()
+        turn_mid.wait_send()
 
 
 def on_square(n, pair, res_mask, *weights):
     side, _, channels = pair.shape
     wide = -(-side // 16) * 16
-    block = (side * side, channels)
-    blocks = pltpu.VMEM((n, *block), jnp.bfloat16)
-    spread_out = pltpu.VMEM((side, wide, channels), jnp.float32)
+    block = pltpu.VMEM((side * side, channels), jnp.bfloat16)
+    blocks = pltpu.VMEM((n, side * side, channels), jnp.bfloat16)
+    positions = pltpu.VMEM((side, wide, channels), jnp.float32)
+    tile = pltpu.VMEM(pair.shape, pair.dtype)
     sems = pltpu.SemaphoreType.DMA((n,))
     in_hbm = pl.BlockSpec(memory_space=pltpu.HBM)
     return pl.pallas_call(
@@ -337,13 +364,13 @@
         out_shape=jax.ShapeDtypeStruct(pair.shape, pair.dtype),
         in_specs=[in_hbm] * (2 + len(weights)),
         out_specs=pl.BlockSpec(memory_space=pltpu.VMEM),
-        scratch_shapes=[pltpu.VMEM(pair.shape, pair.dtype)]
-        + [pltpu.SMEM(res_mask.shape, res_mask.dtype)]
+        scratch_shapes=[tile, pltpu.SMEM(res_mask.shape, res_mask.dtype)]
         + [pltpu.VMEM(w.shape, w.dtype) for w in weights]
-        + [spread_out] * 3
-        + [blocks, blocks, pltpu.VMEM(block, jnp.bfloat16)]
-        + [blocks, pltpu.VMEM(block, jnp.bfloat16), blocks]
+        + [positions] * 3
+        + [tile, blocks, block, blocks]
+        + [block, block, blocks, blocks, block]
         + [pltpu.SemaphoreType.DMA((2 + len(weights),))]
+        + [pltpu.SemaphoreType.DMA((2,))] * 2
         + [sems] * 8,
         compiler_params=pltpu.CompilerParams(
             collective_id=0, has_side_effects=True, vmem_limit_bytes=60 * 2**20

time: 26.5 us -> 21.6 us (0.82)
  Pallas kernels: 24.9 us -> 20 us
    pallas_call x1, Pallas kernels: 24.9 us -> 20 us  [on_square(): pl.pallas_call(functools.partial(kernel, n, side, wide), out_shape=jax.Sh...]
where the time goes in v3:
time: 21.6 us; the launch traced here: 21.4 us
  Pallas kernels  20 us (93%)
  local copies, waits for them, and re-layouts  1.42 us (7%)
    pallas_call x1, Pallas kernels, on_square(): pl.pallas_call(functools.partial(kernel, n, side, wide), out_shape=jax.Sh...  20 us
    unnamed x1, local copies, waits for them, and re-layouts  1.42 us

profile of v3, /device:TPU:0, one launch (start us, length us, event | category | flops | bytes accessed | tf_op | source)
XLA Modules:
  0.0 21.4 jit_solution(11983932069519612334)
XLA Ops:
  0.0 20.0 %shard_map.82 = bf16[12,12,128]{2,1,0:T(8,128)(2,1)} custom-call(bf16[12,12,128]{2,1,0:T(8,128)(2,1)} %pair_hbm.1, s32[48]{0:T(128)} %mask_hbm.1, bf16[128,512]{1,0:T(8,128)(2,1)} %w_ab1_hbm.1, bf16[128,128]{1,0:T(8,128)(2,1)} %w_gate1_hbm.1, bf16[128,128]{1,0:T(8,128)(2,1)} %w_proj1_hbm.1, bf16[128,512]{1,0:T(8,128)(2,1)} %w_ab2_hbm.1, ...), custom_call_target="tpu_custom_call" | custom-call | tf_op jit(solution)/shard_map/pallas_call | solution.py:362
  20.0 1.4 %copy.10 = bf16[12,12,128]{2,1,0:T(8,128)(2,1)} copy(bf16[12,12,128]{2,1,0:T(8,128)(2,1)} %shard_map.82) | data formatting | bytes 73728

commit v4 on v3

--- a/solution.py
+++ b/solution.py
@@ -119,6 +119,11 @@
     padded,
     left_wide,
     right_wide,
+    mask,
+    mask_t,
+    squeeze,
+    squeeze_turned,
+    spread,
     pair_t,
     a1,
     a1_own,
@@ -167,15 +172,22 @@
         loads.append(load)
 
     barrier = pltpu.get_barrier_semaphore()
-    for step in range(1, n * n):
-        other = (row * n + col + step) % (n * n)
+    for step in range(1, n):
         pl.semaphore_signal(
-            barrier, inc=1, device_id=device(other // n, other % n), device_id_type=MESH
+            barrier, inc=1, device_id=device(col, (row + step) % n), device_id_type=MESH
         )
-
-    squeeze = selection((side * side, side * wide), wide, side, False)
-    squeeze_turned = selection((side * side, side * wide), wide, side, True)
-    spread = selection((side * wide, side * side), wide, side, False)
+    for step in range(1, n):
+        pl.semaphore_signal(
+            barrier, inc=1, device_id=device(row, (col + step) % n), device_id_type=MESH
+        )
+
+    @pl.when(jnp.logical_not(mine))
+    def _():
+        pl.semaphore_signal(barrier, inc=1, device_id=device(col, row), device_id_type=MESH)
+
+    squeeze[...] = selection((side * side, side * wide), wide, side, False)
+    squeeze_turned[...] = selection((side * side, side * wide), wide, side, True)
+    spread[...] = selection((side * wide, side * side), wide, side, False)
 
     def tile_mask(rows, cols):
         sublane = lax.broadcasted_iota(jnp.int32, (wide, channels), 0)
@@ -198,7 +210,7 @@
     def gated(normed, w_ab, half, mask):
         hidden = w_ab.shape[1] // 4
         proj = dot(normed, w_ab[:, 2 * half * hidden : 2 * (half + 1) * hidden])
-        return (sigmoid(proj[:, :hidden]) * proj[:, hidden:] * mask).astype(jnp.bfloat16)
+        return (sigmoid(proj[:, :hidden]) * proj[:, hidden:] * mask[...]).astype(jnp.bfloat16)
 
     def finish(values, total, gate, w_proj):
         tri = jnp.concatenate(total, axis=0).astype(jnp.bfloat16).astype(jnp.float32)
@@ -234,7 +246,7 @@
         send(buf.at[slot], buf.at[slot], sems[0].at[0], sems[1].at[slot], row, col).wait_recv()
 
     def widen_block(dst, block):
-        dst[...] = dot(spread, block[...]).reshape(dst.shape)
+        dst[...] = dot(spread[...], block[...]).reshape(dst.shape)
 
     def add_products(total):
         def step(k, total):
@@ -271,15 +283,22 @@
     pair_f = widen(pair_v)
     normed = norm(pair_f)
     loads[1].wait()
-    mask = tile_mask(row, col)
-    mask_t = tile_mask(col, row)
+    mask[...] = tile_mask(row, col)
+    mask_t[...] = tile_mask(col, row)
     loads[2].wait()
     left = gated(normed, w_ab1, 0, mask)
     right = gated(normed, w_ab1, 1, mask)
-    a1_own[...] = dot(squeeze_turned, left).astype(jnp.bfloat16)
-    b1[col] = dot(squeeze_turned, right).astype(jnp.bfloat16)
-
-    pl.semaphore_wait(barrier, n * n - 1)
+    a1_own[...] = dot(squeeze_turned[...], left).astype(jnp.bfloat16)
+    b1[col] = dot(squeeze_turned[...], right).astype(jnp.bfloat16)
+
+    @pl.when(mine)
+    def _():
+        pl.semaphore_wait(barrier, 2 * (n - 1))
+
+    @pl.when(jnp.logical_not(mine))
+    def _():
+        pl.semaphore_wait(barrier, 2 * n - 1)
+
     turn_pair = send(pair_hbm, pair_t, t_send.at[0], t_recv.at[0], col, row)
     stay_pair = pltpu.make_async_copy(pair_hbm, pair_t, t_send.at[0])
 
@@ -303,15 +322,15 @@
 
     pair_f = widen(pair_t)
     normed = norm(pair_f)
-    turned = dot(squeeze_turned, gated(normed, w_ab1, 0, mask_t)).astype(jnp.bfloat16)
-    left_wide[...] = dot(spread, turned).reshape(left_wide.shape)
+    turned = dot(squeeze_turned[...], gated(normed, w_ab1, 0, mask_t)).astype(jnp.bfloat16)
+    left_wide[...] = dot(spread[...], turned).reshape(left_wide.shape)
     loads[3].wait()
     gate = sigmoid(dot(normed, w_gate1[...]))
     total = contract(b1, right_wide, b1_sems, a1, left_wide, a1_sems)
     loads[4].wait()
     middle = finish(pair_f, total, gate, w_proj1)
 
-    mid_own[...] = dot(squeeze, middle).astype(jnp.bfloat16)
+    mid_own[...] = dot(squeeze[...], middle).astype(jnp.bfloat16)
     turn_mid = send(mid_own, mid_t, t_send.at[1], t_recv.at[1], col, row)
 
     @pl.when(jnp.logical_not(mine))
@@ -320,34 +339,34 @@
 
     normed = norm(middle.astype(jnp.float32))
     loads[5].wait()
-    b2_own[...] = dot(squeeze, gated(normed, w_ab2, 1, mask_t)).astype(jnp.bfloat16)
-    a2[col] = dot(squeeze, gated(normed, w_ab2, 0, mask_t)).astype(jnp.bfloat16)
+    b2_own[...] = dot(squeeze[...], gated(normed, w_ab2, 1, mask_t)).astype(jnp.bfloat16)
+    a2[col] = dot(squeeze[...], gated(normed, w_ab2, 0, mask_t)).astype(jnp.bfloat16)
     spread_out(a2.at[col], a2, a2_sems, b2_own, b2, b2_sems)
 
-    @pl.when(jnp.logical_not(mine))
-    def _():
+    for copy in sends[: 2 * (n - 1)]:
+        copy.wait_send()
+
+    @pl.when(jnp.logical_not(mine))
+    def _():
+        turn_pair.wait_send()
+        turn_mid.wait_send()
         turn_mid.wait_recv()
 
     @pl.when(mine)
     def _():
         mid_t[...] = mid_own[...]
 
-    mid_f = dot(spread, mid_t[...])
+    mid_f = dot(spread[...], mid_t[...])
     normed = norm(mid_f)
     right_wide[...] = gated(normed, w_ab2, 1, mask).astype(jnp.float32).reshape(right_wide.shape)
     loads[6].wait()
     gate = sigmoid(dot(normed, w_gate2[...]))
+    for copy in sends[2 * (n - 1) :]:
+        copy.wait_send()
     total = contract(a2, left_wide, a2_sems, b2, right_wide, b2_sems)
     loads[7].wait()
     updated = finish(mid_f, total, gate, w_proj2)
     out_ref[...] = updated.reshape(side, wide, channels)[:, :side, :]
-    for copy in sends:
-        copy.wait_send()
-
-    @pl.when(jnp.logical_not(mine))
-    def _():
-        turn_pair.wait_send()
-        turn_mid.wait_send()
 
 
 def on_square(n, pair, res_mask, *weights):
@@ -361,12 +380,15 @@
     in_hbm = pl.BlockSpec(memory_space=pltpu.HBM)
     return pl.pallas_call(
         functools.partial(kernel, n, side, wide),
-        out_shape=jax.ShapeDtypeStruct(pair.shape, pair.dtype),
+        out_shape=pltpu.VMEM(pair.shape, pair.dtype),
         in_specs=[in_hbm] * (2 + len(weights)),
         out_specs=pl.BlockSpec(memory_space=pltpu.VMEM),
         scratch_shapes=[tile, pltpu.SMEM(res_mask.shape, res_mask.dtype)]
         + [pltpu.VMEM(w.shape, w.dtype) for w in weights]
         + [positions] * 3
+        + [pltpu.VMEM((side * wide, channels), jnp.float32)] * 2
+        + [pltpu.VMEM((side * side, side * wide), jnp.bfloat16)] * 2
+        + [pltpu.VMEM((side * wide, side * side), jnp.bfloat16)]
         + [tile, blocks, block, blocks]
         + [block, block, blocks, blocks, block]
         + [pltpu.SemaphoreType.DMA((2 + len(weights),))]

time: 21.6 us -> 20 us (0.926)
  Pallas kernels: 20 us -> 19.2 us
  local copies, waits for them, and re-layouts: 1.42 us -> 0.62 us
    pallas_call x1, Pallas kernels: 20 us -> 19.2 us  [on_square(): pl.pallas_call(functools.partial(kernel, n, side, wide), out_shape=pltpu....]
    unnamed x1, local copies, waits for them, and re-layouts: 1.42 us -> 0.62 us
where the time goes in v4:
time: 20 us; the launch traced here: 19.8 us
  Pallas kernels  19.2 us (96%)
  local copies, waits for them, and re-layouts  0.62 us (3%)
    pallas_call x1, Pallas kernels, on_square(): pl.pallas_call(functools.partial(kernel, n, side, wide), out_shape=pltpu....  19.2 us
    unnamed x1, local copies, waits for them, and re-layouts  0.62 us

profile of v4, /device:TPU:0, one launch (start us, length us, event | category | flops | bytes accessed | tf_op | source)
XLA Modules:
  0.0 19.8 jit_solution(655701433011326994)
XLA Ops:
  0.0 19.2 %shard_map.82 = bf16[12,12,128]{2,1,0:T(8,128)(2,1)S(1)} custom-call(bf16[12,12,128]{2,1,0:T(8,128)(2,1)} %pair_hbm.1, s32[48]{0:T(128)} %mask_hbm.1, bf16[128,512]{1,0:T(8,128)(2,1)} %w_ab1_hbm.1, bf16[128,128]{1,0:T(8,128)(2,1)} %w_gate1_hbm.1, bf16[128,128]{1,0:T(8,128)(2,1)} %w_proj1_hbm.1, bf16[128,512]{1,0:T(8,128)(2,1)} %w_ab2_hbm.1, ...), custom_call_target="tpu_custom_call" | custom-call | tf_op jit(solution)/shard_map/pallas_call | solution.py:381
  19.2 0.6 %copy.10 = bf16[12,12,128]{2,1,0:T(8,128)(2,1)} copy(bf16[12,12,128]{2,1,0:T(8,128)(2,1)S(1)} %shard_map.82) | data formatting | bytes 73728

commit v5 on v4

--- a/solution.py
+++ b/solution.py
@@ -86,13 +86,13 @@
     return jnp.dot(x, y, preferred_element_type=jnp.float32)
 
 
-def selection(shape, wide, narrow, turned):
-    dense_axis = 0 if shape[0] == narrow * narrow else 1
-    dense = lax.broadcasted_iota(jnp.int32, shape, dense_axis)
-    padded = lax.broadcasted_iota(jnp.int32, shape, 1 - dense_axis)
-    p, q = dense // narrow, dense % narrow
-    place = q * wide + p if turned else p * wide + q
-    return jnp.where(place == padded, 1.0, 0.0).astype(jnp.bfloat16)
+def turning(side, wide):
+    shape = (side * wide, side * wide)
+    to = lax.broadcasted_iota(jnp.int32, shape, 0)
+    source = lax.broadcasted_iota(jnp.int32, shape, 1)
+    q, p = to // wide, to % wide
+    hit = (source == p * wide + q) & (p < side)
+    return jnp.where(hit, 1.0, 0.0).astype(jnp.bfloat16)
 
 
 def kernel(
@@ -121,9 +121,7 @@
     right_wide,
     mask,
     mask_t,
-    squeeze,
-    squeeze_turned,
-    spread,
+    turn,
     pair_t,
     a1,
     a1_own,
@@ -154,6 +152,20 @@
     def device(r, c):
         return {"rows": r, "chan": c // subs, "sub": c % subs}
 
+    barrier = pltpu.get_barrier_semaphore()
+    for step in range(1, n):
+        pl.semaphore_signal(
+            barrier, inc=1, device_id=device(col, (row + step) % n), device_id_type=MESH
+        )
+    for step in range(1, n):
+        pl.semaphore_signal(
+            barrier, inc=1, device_id=device(row, (col + step) % n), device_id_type=MESH
+        )
+
+    @pl.when(jnp.logical_not(mine))
+    def _():
+        pl.semaphore_signal(barrier, inc=1, device_id=device(col, row), device_id_type=MESH)
+
     loads = []
     for place, (src, dst) in enumerate(
         (
@@ -171,23 +183,7 @@
         load.start()
         loads.append(load)
 
-    barrier = pltpu.get_barrier_semaphore()
-    for step in range(1, n):
-        pl.semaphore_signal(
-            barrier, inc=1, device_id=device(col, (row + step) % n), device_id_type=MESH
-        )
-    for step in range(1, n):
-        pl.semaphore_signal(
-            barrier, inc=1, device_id=device(row, (col + step) % n), device_id_type=MESH
-        )
-
-    @pl.when(jnp.logical_not(mine))
-    def _():
-        pl.semaphore_signal(barrier, inc=1, device_id=device(col, row), device_id_type=MESH)
-
-    squeeze[...] = selection((side * side, side * wide), wide, side, False)
-    squeeze_turned[...] = selection((side * side, side * wide), wide, side, True)
-    spread[...] = selection((side * wide, side * side), wide, side, False)
+    turn[...] = turning(side, wide)
 
     def tile_mask(rows, cols):
         sublane = lax.broadcasted_iota(jnp.int32, (wide, channels), 0)
@@ -246,7 +242,7 @@
         send(buf.at[slot], buf.at[slot], sems[0].at[0], sems[1].at[slot], row, col).wait_recv()
 
     def widen_block(dst, block):
-        dst[...] = dot(spread[...], block[...]).reshape(dst.shape)
+        dst[...] = block[...].astype(jnp.float32).reshape(dst.shape)
 
     def add_products(total):
         def step(k, total):
@@ -288,8 +284,8 @@
     loads[2].wait()
     left = gated(normed, w_ab1, 0, mask)
     right = gated(normed, w_ab1, 1, mask)
-    a1_own[...] = dot(squeeze_turned[...], left).astype(jnp.bfloat16)
-    b1[col] = dot(squeeze_turned[...], right).astype(jnp.bfloat16)
+    a1_own[...] = dot(turn[...], left).astype(jnp.bfloat16)
+    b1[col] = dot(turn[...], right).astype(jnp.bfloat16)
 
     @pl.when(mine)
     def _():
@@ -322,15 +318,14 @@
 
     pair_f = widen(pair_t)
     normed = norm(pair_f)
-    turned = dot(squeeze_turned[...], gated(normed, w_ab1, 0, mask_t)).astype(jnp.bfloat16)
-    left_wide[...] = dot(spread[...], turned).reshape(left_wide.shape)
+    left_wide[...] = dot(turn[...], gated(normed, w_ab1, 0, mask_t)).reshape(left_wide.shape)
     loads[3].wait()
     gate = sigmoid(dot(normed, w_gate1[...]))
     total = contract(b1, right_wide, b1_sems, a1, left_wide, a1_sems)
     loads[4].wait()
     middle = finish(pair_f, total, gate, w_proj1)
 
-    mid_own[...] = dot(squeeze[...], middle).astype(jnp.bfloat16)
+    mid_own[...] = middle
     turn_mid = send(mid_own, mid_t, t_send.at[1], t_recv.at[1], col, row)
 
     @pl.when(jnp.logical_not(mine))
@@ -339,8 +334,8 @@
 
     normed = norm(middle.astype(jnp.float32))
     loads[5].wait()
-    b2_own[...] = dot(squeeze[...], gated(normed, w_ab2, 1, mask_t)).astype(jnp.bfloat16)
-    a2[col] = dot(squeeze[...], gated(normed, w_ab2, 0, mask_t)).astype(jnp.bfloat16)
+    b2_own[...] = gated(normed, w_ab2, 1, mask_t)
+    a2[col] = gated(normed, w_ab2, 0, mask_t)
     spread_out(a2.at[col], a2, a2_sems, b2_own, b2, b2_sems)
 
     for copy in sends[: 2 * (n - 1)]:
@@ -356,7 +351,7 @@
     def _():
         mid_t[...] = mid_own[...]
 
-    mid_f = dot(spread[...], mid_t[...])
+    mid_f = mid_t[...].astype(jnp.float32)
     normed = norm(mid_f)
     right_wide[...] = gated(normed, w_ab2, 1, mask).astype(jnp.float32).reshape(right_wide.shape)
     loads[6].wait()
@@ -372,8 +367,8 @@
 def on_square(n, pair, res_mask, *weights):
     side, _, channels = pair.shape
     wide = -(-side // 16) * 16
-    block = pltpu.VMEM((side * side, channels), jnp.bfloat16)
-    blocks = pltpu.VMEM((n, side * side, channels), jnp.bfloat16)
+    block = pltpu.VMEM((side * wide, channels), jnp.bfloat16)
+    blocks = pltpu.VMEM((n, side * wide, channels), jnp.bfloat16)
     positions = pltpu.VMEM((side, wide, channels), jnp.float32)
     tile = pltpu.VMEM(pair.shape, pair.dtype)
     sems = pltpu.SemaphoreType.DMA((n,))
@@ -387,8 +382,7 @@
         + [pltpu.VMEM(w.shape, w.dtype) for w in weights]
         + [positions] * 3
         + [pltpu.VMEM((side * wide, channels), jnp.float32)] * 2
-        + [pltpu.VMEM((side * side, side * wide), jnp.bfloat16)] * 2
-        + [pltpu.VMEM((side * wide, side * side), jnp.bfloat16)]
+        + [pltpu.VMEM((side * wide, side * wide), jnp.bfloat16)]
         + [tile, blocks, block, blocks]
         + [block, block, blocks, blocks, block]
         + [pltpu.SemaphoreType.DMA((2 + len(weights),))]

time: 20 us -> 19.1 us (0.955)
  Pallas kernels: 19.2 us -> 18.3 us
    pallas_call x1, Pallas kernels: 19.2 us -> 18.3 us  [on_square(): pl.pallas_call(functools.partial(kernel, n, side, wide), out_shape=pltpu....]
where the time goes in v5:
time: 19.1 us; the launch traced here: 18.9 us
  Pallas kernels  18.3 us (96%)
  local copies, waits for them, and re-layouts  0.62 us (3%)
    pallas_call x1, Pallas kernels, on_square(): pl.pallas_call(functools.partial(kernel, n, side, wide), out_shape=pltpu....  18.3 us
    unnamed x1, local copies, waits for them, and re-layouts  0.62 us

profile of v5, /device:TPU:0, one launch (start us, length us, event | category | flops | bytes accessed | tf_op | source)
XLA Modules:
  0.0 18.9 jit_solution(2910516436709979100)
XLA Ops:
  0.0 18.3 %shard_map.82 = bf16[12,12,128]{2,1,0:T(8,128)(2,1)S(1)} custom-call(bf16[12,12,128]{2,1,0:T(8,128)(2,1)} %pair_hbm.1, s32[48]{0:T(128)} %mask_hbm.1, bf16[128,512]{1,0:T(8,128)(2,1)} %w_ab1_hbm.1, bf16[128,128]{1,0:T(8,128)(2,1)} %w_gate1_hbm.1, bf16[128,128]{1,0:T(8,128)(2,1)} %w_proj1_hbm.1, bf16[128,512]{1,0:T(8,128)(2,1)} %w_ab2_hbm.1, ...), custom_call_target="tpu_custom_call" | custom-call | tf_op jit(solution)/shard_map/pallas_call | solution.py:376
  18.3 0.6 %copy.10 = bf16[12,12,128]{2,1,0:T(8,128)(2,1)} copy(bf16[12,12,128]{2,1,0:T(8,128)(2,1)S(1)} %shard_map.82) | data formatting | bytes 73728

commit v6 on v5

--- a/solution.py
+++ b/solution.py
@@ -224,6 +224,16 @@
 
     sends = []
 
+    half = side - 8
+    first = lax.broadcasted_iota(jnp.int32, (8, channels), 0) < half
+
+    def pack(x):
+        parts = [x[p * wide : p * wide + 8] for p in range(side)]
+        for p in range(0, side, 2):
+            odd = pltpu.roll(x[(p + 1) * wide + 8 : (p + 2) * wide], half, 0)
+            parts.append(jnp.where(first, x[p * wide + 8 : (p + 1) * wide], odd))
+        return jnp.concatenate(parts, axis=0).astype(jnp.bfloat16)
+
     def spread_out(along, along_buf, along_sems, turn, turn_buf, turn_sems):
         for s in range(1, n):
             copy = send(
@@ -242,7 +252,13 @@
         send(buf.at[slot], buf.at[slot], sems[0].at[0], sems[1].at[slot], row, col).wait_recv()
 
     def widen_block(dst, block):
-        dst[...] = block[...].astype(jnp.float32).reshape(dst.shape)
+        x = block[...].astype(jnp.float32)
+        for p in range(side):
+            dst[p, :8, :] = x[8 * p : 8 * (p + 1)]
+        for p in range(0, side, 2):
+            rest = x[8 * side + 4 * p : 8 * side + 4 * p + 8]
+            dst[p, 8:, :] = rest
+            dst[p + 1, 8:, :] = pltpu.roll(rest, half, 0)
 
     def add_products(total):
         def step(k, total):
@@ -284,8 +300,8 @@
     loads[2].wait()
     left = gated(normed, w_ab1, 0, mask)
     right = gated(normed, w_ab1, 1, mask)
-    a1_own[...] = dot(turn[...], left).astype(jnp.bfloat16)
-    b1[col] = dot(turn[...], right).astype(jnp.bfloat16)
+    a1_own[...] = pack(dot(turn[...], left))
+    b1[col] = pack(dot(turn[...], right))
 
     @pl.when(mine)
     def _():
@@ -325,7 +341,7 @@
     loads[4].wait()
     middle = finish(pair_f, total, gate, w_proj1)
 
-    mid_own[...] = middle
+    mid_own[...] = pack(middle.astype(jnp.float32))
     turn_mid = send(mid_own, mid_t, t_send.at[1], t_recv.at[1], col, row)
 
     @pl.when(jnp.logical_not(mine))
@@ -334,8 +350,8 @@
 
     normed = norm(middle.astype(jnp.float32))
     loads[5].wait()
-    b2_own[...] = gated(normed, w_ab2, 1, mask_t)
-    a2[col] = gated(normed, w_ab2, 0, mask_t)
+    b2_own[...] = pack(gated(normed, w_ab2, 1, mask_t).astype(jnp.float32))
+    a2[col] = pack(gated(normed, w_ab2, 0, mask_t).astype(jnp.float32))
     spread_out(a2.at[col], a2, a2_sems, b2_own, b2, b2_sems)
 
     for copy in sends[: 2 * (n - 1)]:
@@ -351,7 +367,8 @@
     def _():
         mid_t[...] = mid_own[...]
 
-    mid_f = mid_t[...].astype(jnp.float32)
+    widen_block(padded, mid_t)
+    mid_f = padded[...].reshape(side * wide, channels)
     normed = norm(mid_f)
     right_wide[...] = gated(normed, w_ab2, 1, mask).astype(jnp.float32).reshape(right_wide.shape)
     loads[6].wait()
@@ -367,8 +384,8 @@
 def on_square(n, pair, res_mask, *weights):
     side, _, channels = pair.shape
     wide = -(-side // 16) * 16
-    block = pltpu.VMEM((side * wide, channels), jnp.bfloat16)
-    blocks = pltpu.VMEM((n, side * wide, channels), jnp.bfloat16)
+    block = pltpu.VMEM((side * side, channels), jnp.bfloat16)
+    blocks = pltpu.VMEM((n, side * side, channels), jnp.bfloat16)
     positions = pltpu.VMEM((side, wide, channels), jnp.float32)
     tile = pltpu.VMEM(pair.shape, pair.dtype)
     sems = pltpu.SemaphoreType.DMA((n,))
@@ -399,7 +416,7 @@
     square = n == mesh.shape["chan"] * mesh.shape["sub"]
 
     def per_device(pair, *rest):
-        if square and pair.shape[0] == pair.shape[1] and pair.shape[0] <= 16:
+        if square and pair.shape[0] == pair.shape[1] == 12:
             return on_square(n, pair, *rest)
         return on_device(pair, *rest)
 

time: 19.1 us -> 18.4 us (0.963)
  Pallas kernels: 18.3 us -> 17.5 us
    pallas_call x1, Pallas kernels: 18.3 us -> 17.5 us  [on_square(): pl.pallas_call(functools.partial(kernel, n, side, wide), out_shape=pltpu....]
where the time goes in v6:
time: 18.4 us; the launch traced here: 18.2 us
  Pallas kernels  17.5 us (95%)
  local copies, waits for them, and re-layouts  0.62 us (3%)
    pallas_call x1, Pallas kernels, on_square(): pl.pallas_call(functools.partial(kernel, n, side, wide), out_shape=pltpu....  17.5 us
    unnamed x1, local copies, waits for them, and re-layouts  0.62 us

profile of v6, /device:TPU:0, one launch (start us, length us, event | category | flops | bytes accessed | tf_op | source)
XLA Modules:
  0.0 18.2 jit_solution(8852509047463235290)
XLA Ops:
  0.0 17.5 %shard_map.82 = bf16[12,12,128]{2,1,0:T(8,128)(2,1)S(1)} custom-call(bf16[12,12,128]{2,1,0:T(8,128)(2,1)} %pair_hbm.1, s32[48]{0:T(128)} %mask_hbm.1, bf16[128,512]{1,0:T(8,128)(2,1)} %w_ab1_hbm.1, bf16[128,128]{1,0:T(8,128)(2,1)} %w_gate1_hbm.1, bf16[128,128]{1,0:T(8,128)(2,1)} %w_proj1_hbm.1, bf16[128,512]{1,0:T(8,128)(2,1)} %w_ab2_hbm.1, ...), custom_call_target="tpu_custom_call" | custom-call | tf_op jit(solution)/shard_map/pallas_call | solution.py:393
  17.6 0.6 %copy.10 = bf16[12,12,128]{2,1,0:T(8,128)(2,1)} copy(bf16[12,12,128]{2,1,0:T(8,128)(2,1)S(1)} %shard_map.82) | data formatting | bytes 73728

commit v7 on v6

--- a/solution.py
+++ b/solution.py
@@ -234,13 +234,15 @@
             parts.append(jnp.where(first, x[p * wide + 8 : (p + 1) * wide], odd))
         return jnp.concatenate(parts, axis=0).astype(jnp.bfloat16)
 
-    def spread_out(along, along_buf, along_sems, turn, turn_buf, turn_sems):
+    def spread_turned(turn, turn_buf, turn_sems):
         for s in range(1, n):
             copy = send(
                 turn, turn_buf.at[col], turn_sems[0].at[s], turn_sems[1].at[col], (col + s) % n, row
             )
             copy.start()
             sends.append(copy)
+
+    def spread_along(along, along_buf, along_sems):
         for s in range(1, n):
             copy = send(
                 along, along_buf.at[col], along_sems[0].at[s], along_sems[1].at[col], row, (col + s) % n
@@ -322,7 +324,8 @@
     def _():
         stay_pair.start()
 
-    spread_out(b1.at[col], b1, b1_sems, a1_own, a1, a1_sems)
+    spread_turned(a1_own, a1, a1_sems)
+    spread_along(b1.at[col], b1, b1_sems)
 
     @pl.when(jnp.logical_not(mine))
     def _():
@@ -344,15 +347,17 @@
     mid_own[...] = pack(middle.astype(jnp.float32))
     turn_mid = send(mid_own, mid_t, t_send.at[1], t_recv.at[1], col, row)
 
-    @pl.when(jnp.logical_not(mine))
-    def _():
-        turn_mid.start()
-
     normed = norm(middle.astype(jnp.float32))
     loads[5].wait()
     b2_own[...] = pack(gated(normed, w_ab2, 1, mask_t).astype(jnp.float32))
+    spread_turned(b2_own, b2, b2_sems)
+
+    @pl.when(jnp.logical_not(mine))
+    def _():
+        turn_mid.start()
+
     a2[col] = pack(gated(normed, w_ab2, 0, mask_t).astype(jnp.float32))
-    spread_out(a2.at[col], a2, a2_sems, b2_own, b2, b2_sems)
+    spread_along(a2.at[col], a2, a2_sems)
 
     for copy in sends[: 2 * (n - 1)]:
         copy.wait_send()

time: 18.4 us -> 18.3 us (level)
  no operation moved by 1% of the time
where the time goes in v7:
time: 18.3 us; the launch traced here: 18.1 us
  Pallas kernels  17.4 us (95%)
  local copies, waits for them, and re-layouts  0.62 us (3%)
    pallas_call x1, Pallas kernels, on_square(): pl.pallas_call(functools.partial(kernel, n, side, wide), out_shape=pltpu....  17.4 us
    unnamed x1, local copies, waits for them, and re-layouts  0.62 us

profile of v7, /device:TPU:0, one launch (start us, length us, event | category | flops | bytes accessed | tf_op | source)
XLA Modules:
  0.0 18.1 jit_solution(12678744766017374841)
XLA Ops:
  0.0 17.4 %shard_map.82 = bf16[12,12,128]{2,1,0:T(8,128)(2,1)S(1)} custom-call(bf16[12,12,128]{2,1,0:T(8,128)(2,1)} %pair_hbm.1, s32[48]{0:T(128)} %mask_hbm.1, bf16[128,512]{1,0:T(8,128)(2,1)} %w_ab1_hbm.1, bf16[128,128]{1,0:T(8,128)(2,1)} %w_gate1_hbm.1, bf16[128,128]{1,0:T(8,128)(2,1)} %w_proj1_hbm.1, bf16[128,512]{1,0:T(8,128)(2,1)} %w_ab2_hbm.1, ...), custom_call_target="tpu_custom_call" | custom-call | tf_op jit(solution)/shard_map/pallas_call | solution.py:398
  17.5 0.6 %copy.10 = bf16[12,12,128]{2,1,0:T(8,128)(2,1)} copy(bf16[12,12,128]{2,1,0:T(8,128)(2,1)S(1)} %shard_map.82) | data formatting | bytes 73728
